TPU v7x, 32 devices: a whole 2x2x4 slice. The times are simulated.
32 devices in a mesh: sky: 2 (over y), band: 4 (over z), lon: 2 (over x), pol: 2 (over core).
Axes of the slice: x: 2, y: 2, z: 4, core: 2. Of those that a mesh axis runs over, the one named last changes fastest.
Arguments:
- residual_cot: float32 [2, 4, 128, 256], P('pol', 'sky', 'band', 'lon'), parts along dimension 1, may hold values from -6 to 6
- splat_weights: float32 [8, 128, 256], P('sky', 'band', 'lon'), parts along dimension 0, may hold values from 0 to 1
- sample_cycle: int32 [256, 256], P(('sky', 'band'), 'lon'), parts along dimension 0, may hold values from 0 to 1
- sample_pixel: int32 [256, 256], P(('sky', 'band'), 'lon'), parts along dimension 0, may hold values from 0 to 6398
- live_rows: int32 [16], P(('sky', 'band', 'lon')), parts along dimension 0, may hold values from 1 to 32, 128 in all
- table_w: bfloat16 [1536, 4, 3073], P(('band', 'lon', 'pol')), may hold values from -3 to 3
- table_x: bfloat16 [1536, 4, 3073], P(('band', 'lon', 'pol')), may hold values from -3 to 3
- filters: float32 [2, 3072], replicated, may hold values from 0.5 to 2
Outputs:
- gradient: bfloat16 [1536, 4, 2, 3073], P(('band', 'lon', 'pol'), 'sky'), parts along dimension 1
There are 2 independent parts, one for each index of `sky`. A program takes and returns all parts, laid end to end along the dimension named above; an argument that names none is the same for every part. Nothing has to cross between parts.
Inputs may be any that keep to these rules, and one draw needn't show every extreme that they name: `live_rows`: some block has exactly 32 live rows.
All inputs are finite; a program needn't handle non-finite values.
Results may differ from a plain program's by a relative error of at most 0.0059.
Values may be sent and summed in bfloat16 or wider, within the bound.
No kernel may reach another device: no remote copies, remote signals or barrier semaphores. Data moves between devices by JAX's collectives and lax.ppermute only.
A program may use at most 128 MiB of HBM per device.

v0:
```python
import math

import jax
import jax.numpy as jnp
from jax import lax
from jax.sharding import PartitionSpec as P

BAND_CYCLES = 1
NPHI = 12288
M = 3072
RIM = 128


corner_steps = ((0, 0), (0, 1), (1, 0), (1, 1))


def with_halo(array, sides, width, wrap):
    for axis, dim in sides:
        devices, length = (lax.axis_size(axis), array.shape[dim])
        up = [(i, (i + 1) % devices) for i in range(devices if wrap else devices - 1)]
        down = [(j, i) for i, j in up]
        last = lax.slice_in_dim(array, length - width, length, axis=dim)
        first = lax.slice_in_dim(array, 0, width, axis=dim)
        before = lax.ppermute(last, axis, up)
        after = lax.ppermute(first, axis, down)
        array = jnp.concatenate([before, array, after], axis=dim)
    return array


def splat_patch(values, weights, cycle_idx, pix_idx, live_count, ext_width, ext_cycles):
    num_sims = values.shape[0]
    block_rows = 4
    canvas = jnp.zeros((num_sims, ext_cycles * ext_width), jnp.float32)
    steps_needed = (live_count + block_rows - 1) // block_rows

    def add_block(block_step, canvas):
        first_row = block_step * block_rows
        value_rows = lax.dynamic_slice_in_dim(values, first_row, block_rows, 1)
        cycle_rows = lax.dynamic_slice_in_dim(cycle_idx, first_row, block_rows, 0)
        pixel_rows = lax.dynamic_slice_in_dim(pix_idx, first_row, block_rows, 0)
        weight_rows = lax.dynamic_slice_in_dim(weights, first_row, block_rows, 1)
        alive_rows = (first_row + jnp.arange(block_rows, dtype=jnp.int32) < live_count).astype(
            jnp.float32
        )[:, None]
        for corner in range(4):
            cycle_step, pix_step = corner_steps[corner]
            target = ((cycle_rows + cycle_step) * ext_width + pixel_rows + pix_step).reshape(-1)
            amount = (value_rows * (weight_rows[corner] * alive_rows)[None]).reshape(num_sims, -1)
            canvas = canvas.at[:, target].add(amount)
        return canvas

    canvas = lax.fori_loop(0, steps_needed, add_block, canvas)
    return canvas.reshape(num_sims, ext_cycles, ext_width)


def mode_orders(slab_id, quarter, lon_count, pol_count, per_pair):
    positions = jnp.arange(quarter, dtype=jnp.int32)
    per_device = 2 * per_pair
    band_of = positions // (pol_count * per_device)
    pol_of = positions // per_device % pol_count
    side_of = positions // per_pair % 2
    within = positions % per_pair
    owner = (band_of * lon_count + slab_id) * pol_count + pol_of
    pair_id = owner * per_pair + within
    return jnp.where(side_of == 0, pair_id, M - 1 - pair_id)


def cycle_modes(flat_map, first_pixel, orders):
    pixels = first_pixel + jnp.arange(flat_map.shape[1], dtype=jnp.int32)
    turn_index = pixels[:, None] * orders[None, :] % NPHI
    angles = turn_index.astype(jnp.float32) * (2.0 * math.pi / NPHI)
    cos_table = jnp.cos(angles).astype(jnp.bfloat16)
    sin_table = (-jnp.sin(angles)).astype(jnp.bfloat16)
    norm_scale = NPHI ** (-0.5)
    real_part = jnp.dot(flat_map, cos_table, preferred_element_type=jnp.float32) * norm_scale
    imag_part = jnp.dot(flat_map, sin_table, preferred_element_type=jnp.float32) * norm_scale
    return jnp.stack([real_part, imag_part], 1)


def combine(with_w, with_x, pair_id, filters):
    row_width = with_w.shape[-1]
    num_sims = with_w.shape[0] // 8
    positions = jnp.arange(row_width, dtype=jnp.int32)
    first_part = positions < M - pair_id
    with_w = with_w.reshape(2, 2, num_sims, 2, row_width)
    with_x = with_x.reshape(2, 2, num_sims, 2, row_width)
    with_w = jnp.where(first_part, with_w[0], with_w[1])
    with_x = jnp.where(first_part, with_x[0], with_x[1])
    e_real = -(with_w[0, :, 0] - with_x[1, :, 1])
    e_imag = -(with_w[0, :, 1] + with_x[1, :, 0])
    b_real = -(with_w[1, :, 0] + with_x[0, :, 1])
    b_imag = -(with_w[1, :, 1] - with_x[0, :, 0])
    padded = jnp.concatenate([filters, jnp.zeros((2, row_width), jnp.float32)], 1)
    ahead = lax.dynamic_slice_in_dim(padded, pair_id, row_width, 1)
    behind = jnp.concatenate([jnp.zeros((2, 1), jnp.float32), filters], 1)
    filter_rows = jnp.where(first_part, ahead, behind)
    grad_real = filter_rows[0] * e_real + filter_rows[1] * b_real
    grad_imag = filter_rows[0] * e_imag + filter_rows[1] * b_imag
    return jnp.stack([grad_real, grad_imag], 1).astype(jnp.bfloat16)


def body(
    residual_cot, splat_weights, sample_cycle, sample_pixel, live_rows, table_w, table_x, filters
):
    lon_count = lax.axis_size("lon")
    pol_count = lax.axis_size("pol")
    num_sims = residual_cot.shape[1]
    band_cycles = BAND_CYCLES
    pix_dev = NPHI // lon_count
    rim_width = RIM
    ext_width = pix_dev + 2 * rim_width
    ext_cycles = band_cycles + 2
    patch = splat_patch(
        residual_cot[0],
        splat_weights,
        sample_cycle,
        sample_pixel,
        live_rows[0],
        ext_width,
        ext_cycles,
    )
    edges = jnp.concatenate([patch[:, :, :rim_width], patch[:, :, ext_width - rim_width :]], 2)
    beside_all = with_halo(edges, (("lon", 2),), rim_width, True)
    inner = patch[:, :, rim_width : rim_width + pix_dev]
    inner = inner.at[:, :, :rim_width].add(beside_all[:, :, :rim_width])
    inner = inner.at[:, :, pix_dev - rim_width :].add(beside_all[:, :, 3 * rim_width :])
    caps = jnp.concatenate([inner[:, :1], inner[:, ext_cycles - 1 :]], 1)
    beyond = with_halo(caps, (("band", 1),), 1, False)
    own_cycles = inner[:, 1 : ext_cycles - 1]
    own_cycles = own_cycles.at[:, 0].add(beyond[:, 0])
    own_cycles = own_cycles.at[:, band_cycles - 1].add(beyond[:, 3])
    sky_map = own_cycles.astype(jnp.bfloat16)
    per_pair = table_w.shape[0]
    quarter = M // lon_count
    lon_here = lax.axis_index("lon")
    flat_map = sky_map.reshape(num_sims * band_cycles, pix_dev)
    first_pixel = lon_here * pix_dev

    def one_slab(slab_id):
        orders = mode_orders(slab_id, quarter, lon_count, pol_count, per_pair)
        return cycle_modes(flat_map, first_pixel, orders).reshape(num_sims, band_cycles, 2, quarter)

    fourier = lax.psum_scatter(
        lax.map(one_slab, jnp.arange(lax.axis_size("lon") * 1, dtype=jnp.int32)),
        "lon",
        scatter_dimension=0,
        tiled=True,
    )
    fourier = fourier.astype(jnp.bfloat16)
    by_order = lax.all_to_all(
        lax.all_to_all(fourier, "band", split_axis=4, concat_axis=2, tiled=True),
        "pol",
        split_axis=4,
        concat_axis=0,
        tiled=True,
    )
    cycle_total = by_order.shape[2]
    rows_all = by_order.reshape(2, num_sims, cycle_total, 2, 2, per_pair)
    rows_all = jnp.transpose(rows_all, (5, 4, 0, 1, 3, 2)).reshape(
        per_pair, 8 * num_sims, cycle_total
    )
    device_id = (lax.axis_index("band") * lon_count + lon_here) * pol_count + lax.axis_index("pol")
    pair_ids = device_id * per_pair + jnp.arange(per_pair, dtype=jnp.int32)

    def one_pair(operands):
        pair_rows, w_rows, x_rows, pair_id = operands
        with_w = jnp.dot(pair_rows, w_rows, preferred_element_type=jnp.float32)
        with_x = jnp.dot(pair_rows, x_rows, preferred_element_type=jnp.float32)
        return combine(with_w, with_x, pair_id, filters)

    return lax.map(one_pair, (rows_all, table_w, table_x, pair_ids))


def solution(mesh):
    in_specs = (
        P("pol", "sky", "band", "lon"),
        P("sky", "band", "lon"),
        P(("sky", "band"), "lon"),
        P(("sky", "band"), "lon"),
        P(("sky", "band", "lon")),
        P(("band", "lon", "pol"), None, None),
        P(("band", "lon", "pol"), None, None),
        P(),
    )
    out_specs = P(("band", "lon", "pol"), "sky", None, None)
    return jax.shard_map(body, mesh=mesh, in_specs=in_specs, out_specs=out_specs, check_vma=False)
```

profile of v0, /device:TPU:0, one launch (start us, length us, event | category | flops | bytes accessed | tf_op | source)
XLA Modules:
  0.0 1646.7 jit_solution(17356855599760724085)
XLA Ops:
  0.7 1.4 copy.28
  2.1 4.0 broadcast_in_dim.41
  6.1 269.0 %while.37 = (s32[]{:T(128)}, f32[2,19200]{0,1:T(8,128)}, s32[]{:T(128)}, s32[32,128]{1,0:T(8,128)}, s32[32,128]{1,0:T(8,128)}, /*index=5*/f32[2,32,128]{0,2,1:T(...) while((s32[]{:T(128)}, f32[2,19200]{0,1:T(8,128)}, ...), condition=%wide.region_5.6_spmd, body=%wide.region_0.5_spmd.sunk | while | flops 19989 | bytes 131359 | solution.py:52
  8.6 10.6 scatter_fusion
  19.2 10.6 scatter_fusion.1
  29.8 10.6 scatter_fusion.2
  40.3 10.6 scatter_fusion.3
  53.5 10.6 scatter_fusion
  64.0 10.6 scatter_fusion.1
  74.6 10.6 scatter_fusion.2
  85.2 10.6 scatter_fusion.3
  98.3 10.6 scatter_fusion
  108.9 10.6 scatter_fusion.1
  119.4 10.6 scatter_fusion.2
  130.0 10.6 scatter_fusion.3
  143.1 10.6 scatter_fusion
  153.7 10.6 scatter_fusion.1
  164.3 10.6 scatter_fusion.2
  174.8 10.6 scatter_fusion.3
  188.0 10.6 scatter_fusion
  198.5 10.6 scatter_fusion.1
  209.1 10.6 scatter_fusion.2
  219.7 10.6 scatter_fusion.3
  232.8 10.6 scatter_fusion
  243.4 10.6 scatter_fusion.1
  253.9 10.6 scatter_fusion.2
  264.5 10.6 scatter_fusion.3
  275.1 1.2 fusion.63
  276.5 2.1 collective-permute-start.1
  278.5 7.9 slice.191
  286.6 6.3 copy.41
  293.0 94.6 %collective-permute-start.2 = (f32[2,1,6144]{2,1,0:T(1,128)S(1)}, f32[2,1,6144]{2,1,0:T(1,128)S(1)}, u32[]{:S(2)}, u32[]{:S(2)}) collective-permute-start(f32[2,1,6144]{2,1,0:T(1,128)S(1)} %get-tuple-element.340), channel_id=1, source_target_pairs={{0,4},{4,8},{8,12},{1,5},{5,9},{9,13},{2,6},{6,10},{10,14},{3,7},{... | collective-permute-start | bytes 147464 | tf_op jit(solution)/shard_map/ppermute | solution.py:24
  387.6 1.3 collective-permute-start.3
  389.5 4.0 collective-permute-done.3
  393.7 582.6 %while.38 = (s32[]{:T(128)}, f32[2,2,1,2,1536]{4,1,3,2,0:T(2,128)S(1)}, s32[]{:T(128)}, s32[2]{0:T(128)S(1)}, bf16[2,6144]{1,0:T(2,128)(2,1)S(1)}, /*index=5*/s32[]{:T(128)}) while((s32[]{:T(128)}, f32[2,2,1,2,1536]{4,1,3,2,0:T(2,128)S(1)}, s32[]{:T(128)}, s32[2]{0:T(128)S(1)}, bf16[2,6144]{1,0:T(2,128)(2,1)S(1)}, /*index=5*/s32[]{:T(128)}) %tuple.126), condition=%wide.region_7.8_spmd, body=%wide.region_6.7_spmd.sunk | while | flops 273781248 | bytes 215133 | solution.py:144
  395.4 146.0 %fusion.87 = f32[2,1,1536]{2,0,1:T(2,128)S(1)} fusion(bf16[2,6144]{1,0:T(2,128)(2,1)S(1)} %get-tuple-element.579, s32[1536]{0:T(1024)S(1)} %subtract_select_fusion.2, s32[6144]{0:T(1024)S(1)} %iota_add_fusion.3), kind=kOutput, calls=%fused_computation.16.clone.2 | convolution fusion | flops 141560832 | bytes 67584 | tf_op jit(solution)/shard_map/while/body/eval_jaxpr/dot_general | solution.py:76
  541.4 143.7 %fusion.88 = f32[2,1,1536]{2,0,1:T(2,128)S(1)} fusion(bf16[2,6144]{1,0:T(2,128)(2,1)S(1)} %get-tuple-element.579, s32[1536]{0:T(1024)S(1)} %subtract_select_fusion.2, s32[6144]{0:T(1024)S(1)} %iota_add_fusion.3), kind=kOutput, calls=%fused_computation.18.clone.2 | convolution fusion | flops 132123648 | bytes 67584 | tf_op jit(solution)/shard_map/while/body/eval_jaxpr/dot_general | solution.py:75
  686.4 146.0 %fusion.87 = f32[2,1,1536]{2,0,1:T(2,128)S(1)} fusion(bf16[2,6144]{1,0:T(2,128)(2,1)S(1)} %get-tuple-element.579, s32[1536]{0:T(1024)S(1)} %subtract_select_fusion.2, s32[6144]{0:T(1024)S(1)} %iota_add_fusion.3), kind=kOutput, calls=%fused_computation.16.clone.2 | convolution fusion | flops 141560832 | bytes 67584 | tf_op jit(solution)/shard_map/while/body/eval_jaxpr/dot_general | solution.py:76
  832.5 143.7 %fusion.88 = f32[2,1,1536]{2,0,1:T(2,128)S(1)} fusion(bf16[2,6144]{1,0:T(2,128)(2,1)S(1)} %get-tuple-element.579, s32[1536]{0:T(1024)S(1)} %subtract_select_fusion.2, s32[6144]{0:T(1024)S(1)} %iota_add_fusion.3), kind=kOutput, calls=%fused_computation.18.clone.2 | convolution fusion | flops 132123648 | bytes 67584 | tf_op jit(solution)/shard_map/while/body/eval_jaxpr/dot_general | solution.py:75
  976.4 7.2 all-reduce.2
  984.9 1.7 reshape.527
  986.6 3.2 all-to-all-start
  989.9 5.5 all-to-all-done
  995.5 1.7 reshape.528
  997.1 4.9 copy.31
  1002.9 3.7 all_to_all.33
  1008.3 638.2 %while.39 = (s32[]{:T(128)}, bf16[96,2,2,3073]{3,2,1,0:T(2,128)(2,1)}, s32[96]{0:T(128)S(1)}, f32[2,3072]{1,0:T(2,128)S(1)}, bf16[96,16,4]{1,2,0:T(4,128)(2,1)S(...) while((s32[]{:T(128)}, ...), condition=%wide.region_10.11_spmd, body=%wide.region_9.10_spmd.sunk | while | flops 992585 | bytes 3016290 | solution.py:171
  1010.8 1.0 fusion.96
  1022.9 1.0 fusion.94
  1024.0 1.0 fusion.96
  1036.2 1.0 fusion.94
  1044.0 1.0 fusion.96
  1049.5 1.0 fusion.94
  1069.4 1.0 fusion.94
  1070.6 1.0 fusion.96
  1082.7 1.0 fusion.94
  1090.5 1.0 fusion.96
  1096.0 1.0 fusion.94
  1103.8 1.0 fusion.96
  1116.0 1.0 fusion.94
  1117.1 1.0 fusion.96
  1137.1 1.0 fusion.96
  1142.6 1.0 fusion.94
  1150.4 1.0 fusion.96
  (1497 shorter events, 393.8 us)
Async XLA Ops:
  276.3 16.5 %collective-permute-start = (f32[2,3,128]{2,1,0:T(4,128)S(1)}, f32[2,3,128]{2,1,0:T(4,128)S(1)}, u32[]{:S(2)}, u32[]{:S(2)}) collective-permute-start(f32[2,3,128]{2,1,0:T(4,128)S(1)} %copy.43), channel_id=1, source_target_pairs={{0,2},{2,0},{1,3},{3,1},{4,6},{6,4},{5,7},{7,5},{8,10},{10,8},{9,1... | collective-permute-start | bytes 9224 | tf_op jit(solution)/shard_map/ppermute | solution.py:24
  276.5 112.4 %copy-start.1 = (u32[32]{0:T(128)S(1)}, u32[32]{0:T(128)}, u32[]{:S(2)}) copy-start(u32[32]{0:T(128)} %constant.302) | copy-start | bytes 388
  276.5 16.4 collective-permute-start.1
  293.0 96.5 %collective-permute-start.2 = (f32[2,1,6144]{2,1,0:T(1,128)S(1)}, f32[2,1,6144]{2,1,0:T(1,128)S(1)}, u32[]{:S(2)}, u32[]{:S(2)}) collective-permute-start(f32[2,1,6144]{2,1,0:T(1,128)S(1)} %get-tuple-element.340), channel_id=1, source_target_pairs={{0,4},{4,8},{8,12},{1,5},{5,9},{9,13},{2,6},{6,10},{10,14},{3,7},{... | collective-permute-start | bytes 147464 | tf_op jit(solution)/shard_map/ppermute | solution.py:24
  387.6 6.0 collective-permute-start.3
  393.7 614.6 %copy-start = (f32[2,3072]{1,0:T(2,128)S(1)}, f32[2,3072]{1,0:T(2,128)}, u32[]{:S(2)}) copy-start(f32[2,3072]{1,0:T(2,128)} %param.29) | copy-start | bytes 73732
  986.6 8.8 all-to-all-start
where the time goes:
time: 1680 us; the launch traced here: 1650 us
  matrix products  764 us (45%)
  other arithmetic  376 us (22%)
  loops' own time  252 us (15%)
  local copies, waits for them, and re-layouts  132 us (8%)
  starting transfers between devices  101 us (6%)
    dot_general x2, matrix products, cycle_modes(): jnp.dot(flat_map, sin_table, preferred_element_type=jnp.float32)  292 us
    dot_general x2, matrix products, cycle_modes(): jnp.dot(flat_map, cos_table, preferred_element_type=jnp.float32)  287 us
    scatter-add x24, other arithmetic, add_block(): canvas = canvas.at[:, target].add(amount)  254 us
    another operation x1, loops' own time, body(): return lax.map(one_pair, (rows_all, table_w, table_x, pair_ids))  251 us
    ppermute x2, starting transfers between devices, with_halo(): before = lax.ppermute(last, axis, up)  94.6 us
    dot_general x96, matrix products, one_pair(): with_w = jnp.dot(pair_rows, w_rows, preferred_element_type=jnp.float32)  92.4 us
    dot_general x96, matrix products, one_pair(): with_x = jnp.dot(pair_rows, x_rows, preferred_element_type=jnp.float32)  92.4 us
    dynamic_update_slice x96, other arithmetic, body(): return lax.map(one_pair, (rows_all, table_w, table_x, pair_ids))  65.1 us
  transfers between devices with their start and end apart: 5, of which 2 were waited for; matrix products, arithmetic and copies ran while one was open for 1% of the time, Pallas kernels for 0%

commit v1 on v0

v1 whole, which is shorter than its diff:
```python
import functools

import jax
import jax.numpy as jnp
import numpy as np
from jax import lax
from jax.experimental import pallas as pl
from jax.experimental.pallas import tpu as pltpu
from jax.sharding import PartitionSpec as P

BAND_CYCLES = 1
NPHI = 12288
M = 3072
RIM = 128
LANES = 128
FINE = 256
COARSE = NPHI // LANES
TURNS = M // COARSE
HALF = TURNS // 2
EXT_CYCLES = BAND_CYCLES + 2
F32 = jnp.float32
BF16 = jnp.bfloat16
VMEM = pl.BlockSpec(memory_space=pltpu.VMEM)
SMEM = pl.BlockSpec(memory_space=pltpu.SMEM)
HBM = pl.BlockSpec(memory_space=pltpu.HBM)


def split_bf16(array):
    high = array.astype(np.float32).astype(BF16)
    low = (array - high.astype(np.float64)).astype(np.float32).astype(BF16)
    return high, low


def coarse_table(pad_rows):
    row = np.arange(pad_rows)
    step = (2 * row[None, :] + np.arange(2)[:, None]).reshape(-1)
    m0 = np.arange(LANES)
    angle = 2 * np.pi * ((step[None, :] * m0[:, None]) % COARSE) / COARSE
    used = (m0 < COARSE)[:, None]
    high, low = split_bf16(np.concatenate([np.cos(angle) * used, -np.sin(angle) * used], 0))
    return np.concatenate([high, low, high], 1)


def twiddle_table(lon_count, pix_dev):
    l = np.arange(LANES)
    m0 = np.arange(LANES)
    table = np.zeros((lon_count, 2, LANES, LANES), np.float32)
    for j in range(lon_count):
        first = j * pix_dev - RIM
        angle = 2 * np.pi * (((l[None, :] + first) * m0[:, None]) % NPHI) / NPHI
        table[j, 0] = np.cos(angle) * NPHI**-0.5
        table[j, 1] = -np.sin(angle) * NPHI**-0.5
    return table


def fine_table(num_sims):
    l = np.arange(LANES)
    table = np.zeros((2, HALF, num_sims, 2, num_sims, 2, LANES))
    for side in range(2):
        for d in range(HALF):
            m1 = d if side == 0 else TURNS - 1 - d
            angle = 2 * np.pi * ((l * m1) % LANES) / LANES
            for s in range(num_sims):
                table[side, d, s, 0, s, 0] = np.cos(angle)
                table[side, d, s, 0, s, 1] = np.sin(angle)
                table[side, d, s, 1, s, 0] = -np.sin(angle)
                table[side, d, s, 1, s, 1] = np.cos(angle)
    return split_bf16(table.reshape(4 * HALF * num_sims, 2 * num_sims * LANES))[0]


def analyse_kernel(
    live_ref, value_ref, weight_ref, cycle_ref, pixel_ref, coarse_hbm, twiddle_hbm, fine_hbm,
    out_ref, amount, index, left, right, coarse_ref, twiddle_ref, fine_ref, sems, *, pad_rows,
):
    tables = [
        pltpu.make_async_copy(coarse_hbm, coarse_ref, sems.at[0]),
        pltpu.make_async_copy(twiddle_hbm.at[lax.axis_index("lon")], twiddle_ref, sems.at[1]),
        pltpu.make_async_copy(fine_hbm, fine_ref, sems.at[2]),
    ]
    for copy in tables:
        copy.start()
    num_sims, rows = value_ref.shape[1:3]
    maps = num_sims * EXT_CYCLES
    alive = lax.broadcasted_iota(jnp.int32, (rows, LANES), 0) < live_ref[0]
    cycle = cycle_ref[...]
    for dp in range(2):
        pixel = pixel_ref[...] + dp
        index[0, dp] = (pixel >> 8).astype(F32)
        index[1, dp] = (pixel & (FINE - 1)).astype(F32)
        for s in range(num_sims):
            value = jnp.where(alive, value_ref[0, s], 0.0)
            here = value * weight_ref[dp]
            above = value * weight_ref[2 + dp]
            for c in range(EXT_CYCLES):
                amount[s * EXT_CYCLES + c, dp] = jnp.where(
                    cycle == c, here, jnp.where(cycle == c - 1, above, 0.0)
                )
    row_at = lax.broadcasted_iota(jnp.int32, (pad_rows, LANES), 0).astype(F32).astype(BF16)
    fine_at = lax.broadcasted_iota(jnp.int32, (FINE, LANES), 0).astype(F32).astype(BF16)
    one, zero = jnp.ones((), BF16), jnp.zeros((), BF16)

    def all_rows(ref, n, dp, k, count):
        row = jnp.broadcast_to(ref[n, dp, k : k + 1, :], (16, LANES)).astype(BF16)
        return jnp.concatenate([row] * (count // 16), 0)

    for k in range(rows):
        for dp in range(2):
            here = slice(FINE * k + LANES * dp, FINE * k + LANES * (dp + 1))
            hit = row_at == all_rows(index, 0, dp, k, pad_rows)
            for n in range(maps):
                left[n * pad_rows : (n + 1) * pad_rows, here] = jnp.where(
                    hit, all_rows(amount, n, dp, k, pad_rows), zero
                )
            right[:, here] = jnp.where(fine_at == all_rows(index, 1, dp, k, FINE), one, zero)
    dims = (((1,), (1,)), ((), ()))
    canvas = lax.dot_general(left[...], right[...], dims, preferred_element_type=F32)
    canvas = jnp.concatenate(
        [
            jnp.concatenate(
                [
                    canvas[n * pad_rows : (n + 1) * pad_rows, b * LANES : (b + 1) * LANES]
                    for n in range(maps)
                ],
                1,
            )
            for b in range(2)
        ],
        0,
    )
    high = canvas.astype(BF16)
    low = (canvas - high.astype(F32)).astype(BF16)
    for copy in tables:
        copy.wait()
    coarse = jnp.dot(
        coarse_ref[...], jnp.concatenate([high, high, low], 0), preferred_element_type=F32
    )
    turn_re, turn_im = twiddle_ref[0], twiddle_ref[1]
    blocks = []
    for c in range(EXT_CYCLES):
        lanes = []
        for s in range(num_sims):
            n = s * EXT_CYCLES + c
            real = coarse[:LANES, n * LANES : (n + 1) * LANES]
            imag = coarse[LANES:, n * LANES : (n + 1) * LANES]
            lanes += [real * turn_re - imag * turn_im, real * turn_im + imag * turn_re]
        blocks.append(jnp.concatenate(lanes, 1))
    turned = jnp.concatenate(blocks, 0).astype(BF16)
    modes = lax.dot_general(fine_ref[...], turned, dims, preferred_element_type=F32)
    half = modes.shape[0] // 2
    modes = jnp.concatenate([modes[:half], modes[half:]], 1).astype(BF16)
    out_ref[...] = modes.reshape(out_ref.shape)


def analyse(live_rows, values, weights, cycle, pixel, pix_dev, lon_count):
    num_sims, rows = values.shape[1:3]
    pad_rows = -(-(pix_dev + 2 * RIM) // FINE // 16) * 16
    maps = num_sims * EXT_CYCLES
    coarse, fine = coarse_table(pad_rows), fine_table(num_sims)
    twiddle = twiddle_table(lon_count, pix_dev)
    out_shape = (HALF, 2 * num_sims, 2 * EXT_CYCLES * LANES)

    def whole(shape):
        return pl.BlockSpec(shape, lambda i: (0,) * len(shape))

    return pl.pallas_call(
        functools.partial(analyse_kernel, pad_rows=pad_rows),
        grid=(1,),
        in_specs=[
            SMEM,
            whole(values.shape),
            whole(weights.shape),
            whole(cycle.shape),
            whole(pixel.shape),
            HBM,
            HBM,
            HBM,
        ],
        out_specs=whole(out_shape),
        scratch_shapes=[
            pltpu.VMEM((maps, 2, rows, LANES), F32),
            pltpu.VMEM((2, 2, rows, LANES), F32),
            pltpu.VMEM((maps * pad_rows, rows * FINE), BF16),
            pltpu.VMEM((FINE, rows * FINE), BF16),
            pltpu.VMEM(coarse.shape, BF16),
            pltpu.VMEM(twiddle.shape[1:], F32),
            pltpu.VMEM(fine.shape, BF16),
            pltpu.SemaphoreType.DMA((3,)),
        ],
        out_shape=jax.ShapeDtypeStruct(out_shape, BF16),
        compiler_params=pltpu.CompilerParams(vmem_limit_bytes=56 << 20),
    )(
        live_rows, values, weights, cycle, pixel,
        jnp.asarray(coarse), jnp.asarray(twiddle), jnp.asarray(fine),
    )


def first_pair_here(per_pair):
    place = lax.axis_index("band") * lax.axis_size("lon") + lax.axis_index("lon")
    return (place * lax.axis_size("pol") + lax.axis_index("pol")) * per_pair


def spread_kernel(filters_ref, out_ref, *, per_pair):
    wide = out_ref.shape[3]
    first_pair = first_pair_here(per_pair)
    second = lax.broadcasted_iota(jnp.int32, (8, wide), 0) // 4
    for f in range(2):
        full = jnp.concatenate([filters_ref[f : f + 1, :], jnp.zeros((1, wide - M), F32)], 1)
        full = jnp.broadcast_to(full, (8, wide))
        ahead = jnp.where(second == 1, pltpu.roll(full, wide - 1, 1), full)
        out_ref[0, f] = pltpu.roll(ahead, wide - first_pair, 1)
        out_ref[1, f] = pltpu.roll(full, 1, 1)


def spread_filters(filters, per_pair):
    wide = M + FINE + -(-per_pair // LANES) * LANES
    return pl.pallas_call(
        functools.partial(spread_kernel, per_pair=per_pair),
        in_specs=[VMEM],
        out_specs=VMEM,
        out_shape=jax.ShapeDtypeStruct((2, 2, 8, wide), F32),
        compiler_params=pltpu.CompilerParams(vmem_limit_bytes=8 << 20),
        cost_estimate=pl.CostEstimate(flops=400 * wide, bytes_accessed=160 * wide, transcendentals=0),
    )(filters)


def grouping(per_pair, cycles):
    group = 2
    while per_pair % (2 * group) == 0 and 2 * group * cycles <= LANES:
        group *= 2
    return group, -(-group * cycles // LANES) * LANES


def swap_parts(array):
    even = lax.broadcasted_iota(jnp.int32, array.shape, 0) % 2 == 0
    return jnp.where(even, pltpu.roll(array, 7, 0), pltpu.roll(array, 1, 0))


def contract_kernel(
    modes_ref, spread_ref, w_hbm, x_hbm, out_ref, modes, factors, held, w_ref, x_ref, sems, *, direct
):
    per_pair, cycles, row_width = w_ref.shape
    group, pad_depth = grouping(per_pair, cycles)
    groups, depth, half = per_pair // group, group * cycles, 4 * group
    tables = []
    for g in range(groups):
        part = pl.ds(g * group, group)
        tables.append(
            [
                pltpu.make_async_copy(w_hbm.at[part], w_ref.at[part], sems.at[g, 0]),
                pltpu.make_async_copy(x_hbm.at[part], x_ref.at[part], sems.at[g, 1]),
            ]
        )
        for copy in tables[-1]:
            copy.start()
    for comp in range(2):
        for side in range(2):
            for r in range(cycles):
                if direct:
                    total = jnp.zeros((4, LANES), F32)
                    lons = modes_ref.shape[0] // (2 * cycles)
                    for c in range(EXT_CYCLES):
                        band = r + 1 - c
                        if 0 <= band < cycles:
                            for j in range(lons):
                                lane = (side * EXT_CYCLES + c) * LANES
                                total += modes_ref[
                                    (band * lons + j) * 2 + comp, :, lane : lane + LANES
                                ].astype(F32)
                    total = total.astype(BF16).astype(F32)
                    total = jnp.concatenate([total, total], 0)
                else:
                    total = modes_ref[comp, side, r]
                modes[comp, side, r] = total

    lane = lax.broadcasted_iota(jnp.int32, (8, LANES), 1)
    sign = jnp.where(lax.broadcasted_iota(jnp.int32, (8, pad_depth), 0) % 2 == 0, 1.0, -1.0)
    own = (
        lax.broadcasted_iota(jnp.int32, (half, pad_depth), 0) // 4
        == lax.broadcasted_iota(jnp.int32, (half, pad_depth), 1) // cycles
    )
    copies = []
    for g in range(groups):
        for side in range(2):
            spread = []
            for comp in range(2):
                parts = []
                for first in range(0, pad_depth, LANES):
                    at = jnp.minimum(g * group + (first + lane) // cycles, per_pair - 1)
                    if direct and side == 1:
                        at = per_pair - 1 - at
                    value = jnp.zeros((8, LANES), F32)
                    for r in range(cycles):
                        taken = jnp.take_along_axis(
                            modes[comp, side, r], at, axis=1, mode="promise_in_bounds"
                        )
                        value = jnp.where((first + lane) % cycles == r, taken, value)
                    parts.append(value)
                spread.append(jnp.concatenate(parts, 1) if len(parts) > 1 else parts[0])
            q, u = spread
            pairs = ((-q, sign * swap_parts(u)), (-u, -sign * swap_parts(q)))
            for f, bases in enumerate(pairs):
                for n, base in enumerate(bases):
                    full = jnp.where(own, jnp.tile(base, (half // 8, 1)), 0.0).astype(BF16)
                    factors[
                        g, side, f * half : (f + 1) * half, n * pad_depth : (n + 1) * pad_depth
                    ] = full

    for g in range(groups):
        first_pair = first_pair_here(per_pair) + g * group
        for copy in tables[g]:
            copy.wait()

        def table_rows(cols):
            rows = []
            for ref in (w_ref, x_ref):
                rows.append(ref[g * group : (g + 1) * group, :, cols].reshape(depth, -1))
                if depth < pad_depth:
                    rows.append(jnp.zeros((pad_depth - depth, rows[0].shape[1]), BF16))
            return jnp.concatenate(rows, 0)

        def filtered(rows, side, start, width):
            both = jnp.dot(factors[g, side], rows, preferred_element_type=F32)
            near = 1 - side
            total = []
            source = [spread_ref[side, f, :, pl.ds(start, FINE + LANES)] for f in range(2)]
            for a in range(half // 8):
                shift = 2 * a + g * group
                e, b = (
                    pltpu.roll(source[f], (FINE + LANES) - shift * near, 1)[:, :width] for f in range(2)
                )
                total.append(e * both[8 * a : 8 * a + 8] + b * both[half + 8 * a : half + 8 * a + 8])
            return jnp.concatenate(total, 0)

        def put(total, cols):
            held[g, :, :, :, cols] = total.astype(BF16).reshape(group, 2, 2, -1)

        for start in range(0, row_width, FINE):
            cols = slice(start, min(start + FINE, row_width))
            side = (start >= M - first_pair).astype(jnp.int32)
            put(filtered(table_rows(cols), side, start, cols.stop - start), cols)
        start = pl.multiple_of((M - 1 - first_pair) // FINE * FINE, FINE)
        cols = pl.ds(start, FINE)
        rows = table_rows(cols)
        pair = first_pair + lax.broadcasted_iota(jnp.int32, (half, FINE), 0) // 4
        at = start + lax.broadcasted_iota(jnp.int32, (half, FINE), 1)
        near, far = (filtered(rows, side, start, FINE) for side in range(2))
        put(jnp.where(at < M - pair, near, far), cols)
        copy = pltpu.make_async_copy(
            held.at[g], out_ref.at[pl.ds(g * group, group)], sems.at[g, 2]
        )
        copy.start()
        copies.append(copy)
    for copy in copies:
        copy.wait()


def contract(modes, spread, table_w, table_x, direct):
    per_pair, cycles, row_width = table_w.shape
    group, pad_depth = grouping(per_pair, cycles)
    groups = per_pair // group
    return pl.pallas_call(
        functools.partial(contract_kernel, direct=direct),
        in_specs=[VMEM, VMEM, HBM, HBM],
        out_specs=HBM,
        out_shape=jax.ShapeDtypeStruct((per_pair, 2, 2, row_width), BF16),
        scratch_shapes=[
            pltpu.VMEM((2, 2, cycles, 8, LANES), F32),
            pltpu.VMEM((groups, 2, 8 * group, 2 * pad_depth), BF16),
            pltpu.VMEM((groups, group, 2, 2, row_width), BF16),
            pltpu.VMEM(table_w.shape, BF16),
            pltpu.VMEM(table_x.shape, BF16),
            pltpu.SemaphoreType.DMA((groups, 3)),
        ],
        compiler_params=pltpu.CompilerParams(vmem_limit_bytes=56 << 20),
    )(modes, spread, table_w, table_x)


def by_owner(payload, per_pair):
    split = COARSE // per_pair
    parts = payload.reshape(HALF, 4, 2, EXT_CYCLES, LANES)[..., :COARSE]
    parts = jnp.stack([parts[:, :, 0], parts[:, :, 1, :, ::-1]], 2)
    parts = parts.reshape(HALF, 4, 2, EXT_CYCLES, split, per_pair)
    parts = jnp.transpose(parts, (0, 4, 1, 2, 3, 5))
    return parts.reshape(HALF * split, 4, 2, EXT_CYCLES, per_pair)


def sum_sources(received, bands, lons):
    per_pair = received.shape[-1]
    parts = received.astype(F32).reshape(bands, lons, 2, 4, 2, EXT_CYCLES, per_pair).sum(1)
    parts = jnp.pad(parts, ((1, 1), (0, 0), (0, 0), (0, 0), (0, 0), (0, 0)))
    total = sum(parts[2 - c : 2 - c + bands, :, :, :, c] for c in range(EXT_CYCLES))
    total = jnp.transpose(total, (1, 3, 0, 2, 4)).astype(BF16).astype(F32)
    total = jnp.concatenate([total, total], 3)
    return jnp.pad(total, ((0, 0),) * 4 + ((0, LANES - per_pair),))


def body(
    residual_cot, splat_weights, sample_cycle, sample_pixel, live_rows, table_w, table_x, filters
):
    bands = lax.axis_size("band")
    lons = lax.axis_size("lon")
    owners = ("band", "lon", "pol")
    per_pair = table_w.shape[0]
    payload = analyse(
        live_rows, residual_cot, splat_weights, sample_cycle, sample_pixel, NPHI // lons, lons
    )
    direct = per_pair == COARSE
    if not direct:
        payload = by_owner(payload, per_pair)
    modes = lax.all_to_all(payload, owners, 0, 0, tiled=True)
    if not direct:
        modes = sum_sources(modes, bands, lons)
    spread = spread_filters(filters, per_pair)
    return contract(modes, spread, table_w, table_x, direct)


def solution(mesh):
    in_specs = (
        P("pol", "sky", "band", "lon"),
        P("sky", "band", "lon"),
        P(("sky", "band"), "lon"),
        P(("sky", "band"), "lon"),
        P(("sky", "band", "lon")),
        P(("band", "lon", "pol"), None, None),
        P(("band", "lon", "pol"), None, None),
        P(),
    )
    out_specs = P(("band", "lon", "pol"), "sky", None, None)
    return jax.shard_map(body, mesh=mesh, in_specs=in_specs, out_specs=out_specs, check_vma=False)
```

time: 1680 us -> 28.8 us (0.02); the launches traced: 1650 us -> 28.5 us
  matrix products: 764 us -> 0 us
  other arithmetic: 376 us -> 0 us
  loops' own time: 252 us -> 0 us
  local copies, waits for them, and re-layouts: 132 us -> 2.13 us
  starting transfers between devices: 101 us -> 7.37 us
    dot_general x196 -> x0, matrix products: 764 us -> none  [the longest x2 292 us: cycle_modes(): jnp.dot(flat_map, sin_table, preferred_element_type=jnp.float32)]
    scatter-add x26 -> x0, other arithmetic: 254 us -> none  [the longest x24 254 us: add_block(): canvas = canvas.at[:, target].add(amount)]
    another operation x3 -> x0, loops' own time: 252 us -> none  [the longest x1 251 us: body(): return lax.map(one_pair, (rows_all, table_w, table_x, pair_ids))]
    ppermute x4 -> x0, starting transfers between devices: 98 us -> none  [the longest x2 94.6 us: with_halo(): before = lax.ppermute(last, axis, up)]
    dynamic_update_slice x98 -> x0, other arithmetic: 65.1 us -> none  [the longest x96 65.1 us: body(): return lax.map(one_pair, (rows_all, table_w, table_x, pair_ids))]
    dynamic_slice x98 -> x0, local copies, waits for them, and re-layouts: 63.2 us -> none  [the longest x96 62 us: body(): return lax.map(one_pair, (rows_all, table_w, table_x, pair_ids))]
    squeeze x384 -> x0, local copies, waits for them, and re-layouts: 25.5 us -> none  [the longest x192 12.7 us: combine(): with_x = jnp.where(first_part, with_x[0], with_x[1])]
    select_n x206 -> x0, other arithmetic: 24.9 us -> none  [the longest x96 12.1 us: combine(): filter_rows = jnp.where(first_part, ahead, behind)]
  transfers between devices with their start and end apart: 5 -> 1, of which waited for: 2 -> 1; matrix products, arithmetic and copies ran while one was open for 1% -> 0% of each run, Pallas kernels for 0% -> 1%
where the time goes in v1:
time: 28.8 us; the launch traced here: 28.5 us
  Pallas kernels  12.7 us (44%)
  starting transfers between devices  7.37 us (26%)
  waiting for transfers between devices  5.58 us (19%)
  local copies, waits for them, and re-layouts  2.13 us (7%)
  between operations  0.69 us (2%)
    pallas_call x1, Pallas kernels, contract(): pl.pallas_call(functools.partial(contract_kernel, direct=direct), in_spec...  8.21 us
    all_to_all x1, starting transfers between devices, body(): modes = lax.all_to_all(payload, owners, 0, 0, tiled=True)  7.37 us
    all_to_all x1, waiting for transfers between devices, body(): modes = lax.all_to_all(payload, owners, 0, 0, tiled=True)  5.58 us
    pallas_call x1, Pallas kernels, analyse(): pl.pallas_call(functools.partial(analyse_kernel, pad_rows=pad_rows), grid...  4.22 us
    unnamed x6, local copies, waits for them, and re-layouts  2.13 us
  transfers between devices with their start and end apart: 1, of which 1 were waited for; matrix products, arithmetic and copies ran while one was open for 0% of the time, Pallas kernels for 1%

profile of v1, /device:TPU:0, one launch (start us, length us, event | category | flops | bytes accessed | tf_op | source)
XLA Modules:
  0.0 28.5 jit_solution(12301718650274412443)
XLA Ops:
  0.7 4.2 %shard_map.109 = bf16[16,4,768]{2,1,0:T(4,128)(2,1)} custom-call(s32[1]{0:T(128)S(6)} %copy.12.live_ref, f32[1,2,32,128]{3,2,1,0:T(8,128)} %value_ref.1, f32[4,32,128]{2,1,0:T(8,128)} %weight_ref.1, s32[32,128]{1,0:T(8,128)} %cycle_ref.1, s32[32,128]{1,0:T(8,128)} %pixel_ref.1, bf16[256,192]{1,0:T(8,128)(2,1)} %constant.6.clone.coarse_hbm, ...), custom_call_target="tpu_custom_call" | custom-call | tf_op jit(solution)/shard_map/pallas_call | solution.py:165
  4.9 7.4 %all-to-all-start = ((bf16[16,4,768]{2,1,0:T(4,128)(2,1)}), bf16[16,4,768]{2,1,0:T(4,128)(2,1)S(1)}, u32[]{:S(2)}, u32[]{:S(2)}) async-start(bf16[16,4,768]{2,1,0:T(4,128)(2,1)} %shard_map.109), calls=%async_computation | async-start | bytes 196608 | tf_op jit(solution)/shard_map/all_to_all | solution.py:410
  12.3 0.0 copy-start.1
  12.3 0.7 %copy-done.1 = f32[2,3072]{1,0:T(2,128)S(1)} copy-done((f32[2,3072]{1,0:T(2,128)S(1)}, f32[2,3072]{1,0:T(2,128)}, u32[]{:S(2)}) %copy-start.1) | copy-done | bytes 24600
  13.0 0.3 %shard_map.110.spread_ref = f32[2,2,8,3456]{3,2,1,0:T(8,128)S(1)} custom-call(f32[2,3072]{1,0:T(2,128)S(1)} %copy-done.1), custom_call_target="tpu_custom_call" | custom-call | flops 1382400 | bytes 552960 | tf_op jit(solution)/shard_map/pallas_call | solution.py:216
  13.3 0.0 copy-start
  13.3 0.8 %copy-done = f32[2,2,8,3456]{3,2,1,0:T(8,128)} copy-done((f32[2,2,8,3456]{3,2,1,0:T(8,128)}, f32[2,2,8,3456]{3,2,1,0:T(8,128)S(1)}, u32[]{:S(2)}) %copy-start) | copy-done | bytes 442392
  14.1 5.6 %all-to-all-done.modes_ref = bf16[16,4,768]{2,1,0:T(4,128)(2,1)S(1)} async-done(((bf16[16,4,768]{2,1,0:T(4,128)(2,1)}), bf16[16,4,768]{2,1,0:T(4,128)(2,1)S(1)}, u32[]{:S(2)}, u32[]{:S(2)}) %all-to-all-start) | async-done | bytes 98336 | tf_op jit(solution)/shard_map/all_to_all | solution.py:410
  19.7 0.0 copy-start.2
  19.7 0.6 %copy-done.2 = bf16[16,4,768]{2,1,0:T(4,128)(2,1)} copy-done((bf16[16,4,768]{2,1,0:T(4,128)(2,1)}, bf16[16,4,768]{2,1,0:T(4,128)(2,1)S(1)}, u32[]{:S(2)}) %copy-start.2) | copy-done | bytes 98328
  20.3 8.2 %shard_map.111 = bf16[96,2,2,3073]{3,2,1,0:T(2,128)(2,1)} custom-call(bf16[16,4,768]{2,1,0:T(4,128)(2,1)} %copy-done.2, f32[2,2,8,3456]{3,2,1,0:T(8,128)} %copy-done, bf16[96,4,3073]{2,1,0:T(4,128)(2,1)} %w_hbm.1, bf16[96,4,3073]{2,1,0:T(4,128)(2,1)} %x_hbm.1), custom_call_target="tpu_custom_call" | custom-call | tf_op jit(solution)/shard_map/pallas_call | solution.py:361
Async XLA Ops:
  4.9 14.8 %all-to-all-start = ((bf16[16,4,768]{2,1,0:T(4,128)(2,1)}), bf16[16,4,768]{2,1,0:T(4,128)(2,1)S(1)}, u32[]{:S(2)}, u32[]{:S(2)}) async-start(bf16[16,4,768]{2,1,0:T(4,128)(2,1)} %shard_map.109), calls=%async_computation | async-start | bytes 196608 | tf_op jit(solution)/shard_map/all_to_all | solution.py:410
  12.3 0.7 %copy-start.1 = (f32[2,3072]{1,0:T(2,128)S(1)}, f32[2,3072]{1,0:T(2,128)}, u32[]{:S(2)}) copy-start(f32[2,3072]{1,0:T(2,128)} %filters_ref.1) | copy-start | bytes 73732
  13.3 0.8 %copy-start = (f32[2,2,8,3456]{3,2,1,0:T(8,128)}, f32[2,2,8,3456]{3,2,1,0:T(8,128)S(1)}, u32[]{:S(2)}) copy-start(f32[2,2,8,3456]{3,2,1,0:T(8,128)S(1)} %shard_map.110.spread_ref) | copy-start | bytes 1327108
  19.7 0.6 %copy-start.2 = (bf16[16,4,768]{2,1,0:T(4,128)(2,1)}, bf16[16,4,768]{2,1,0:T(4,128)(2,1)S(1)}, u32[]{:S(2)}) copy-start(bf16[16,4,768]{2,1,0:T(4,128)(2,1)S(1)} %all-to-all-done.modes_ref) | copy-start | bytes 294916

commit v2 on v1

--- a/solution.py
+++ b/solution.py
@@ -14,6 +14,7 @@
 RIM = 128
 LANES = 128
 FINE = 256
+PIECE = 1024
 COARSE = NPHI // LANES
 TURNS = M // COARSE
 HALF = TURNS // 2
@@ -199,27 +200,40 @@
     return (place * lax.axis_size("pol") + lax.axis_index("pol")) * per_pair
 
 
-def spread_kernel(filters_ref, out_ref, *, per_pair):
-    wide = out_ref.shape[3]
-    first_pair = first_pair_here(per_pair)
-    second = lax.broadcasted_iota(jnp.int32, (8, wide), 0) // 4
+def spread_kernel(filters_ref, out_ref):
+    groups, _, group, wide = out_ref.shape
+    first_pair = first_pair_here(groups * group)
+    at = lax.broadcasted_iota(jnp.int32, (8, wide), 1)
+    row = lax.broadcasted_iota(jnp.int32, (8, wide), 0)
     for f in range(2):
         full = jnp.concatenate([filters_ref[f : f + 1, :], jnp.zeros((1, wide - M), F32)], 1)
         full = jnp.broadcast_to(full, (8, wide))
-        ahead = jnp.where(second == 1, pltpu.roll(full, wide - 1, 1), full)
-        out_ref[0, f] = pltpu.roll(ahead, wide - first_pair, 1)
-        out_ref[1, f] = pltpu.roll(full, 1, 1)
-
-
-def spread_filters(filters, per_pair):
-    wide = M + FINE + -(-per_pair // LANES) * LANES
+        behind = pltpu.roll(full, 1, 1)
+        ahead = full
+        for bit in (1, 2, 4):
+            ahead = jnp.where(row & bit != 0, pltpu.roll(ahead, wide - bit, 1), ahead)
+        ahead = pltpu.roll(ahead, wide - first_pair, 1)
+        for g in range(groups):
+            for a in range(0, group, 8):
+                first = g * group + a
+                here = pltpu.roll(ahead, wide - first, 1) if first else ahead
+                here = jnp.where(at < M - first_pair - first - row, here, behind)
+                count = min(8, group - a)
+                out_ref[g, f, a : a + count, :] = here[:count]
+
+
+def spread_filters(filters, per_pair, cycles):
+    group = grouping(per_pair, cycles)[0]
+    wide = -(-(M + 1) // LANES) * LANES
     return pl.pallas_call(
-        functools.partial(spread_kernel, per_pair=per_pair),
+        spread_kernel,
         in_specs=[VMEM],
         out_specs=VMEM,
-        out_shape=jax.ShapeDtypeStruct((2, 2, 8, wide), F32),
+        out_shape=jax.ShapeDtypeStruct((per_pair // group, 2, group, wide), F32),
         compiler_params=pltpu.CompilerParams(vmem_limit_bytes=8 << 20),
-        cost_estimate=pl.CostEstimate(flops=400 * wide, bytes_accessed=160 * wide, transcendentals=0),
+        cost_estimate=pl.CostEstimate(
+            flops=20 * per_pair * wide, bytes_accessed=8 * per_pair * wide, transcendentals=0
+        ),
     )(filters)
 
 
@@ -236,7 +250,8 @@
 
 
 def contract_kernel(
-    modes_ref, spread_ref, w_hbm, x_hbm, out_ref, modes, factors, held, w_ref, x_ref, sems, *, direct
+    modes_ref, spread_ref, w_hbm, x_hbm, out_ref,
+    modes, factors, held, w_ref, x_ref, sems, *, direct,
 ):
     per_pair, cycles, row_width = w_ref.shape
     group, pad_depth = grouping(per_pair, cycles)
@@ -318,38 +333,52 @@
                     rows.append(jnp.zeros((pad_depth - depth, rows[0].shape[1]), BF16))
             return jnp.concatenate(rows, 0)
 
-        def filtered(rows, side, start, width):
+        def filtered(rows, side, cols):
             both = jnp.dot(factors[g, side], rows, preferred_element_type=F32)
-            near = 1 - side
+            width = both.shape[1]
             total = []
-            source = [spread_ref[side, f, :, pl.ds(start, FINE + LANES)] for f in range(2)]
             for a in range(half // 8):
-                shift = 2 * a + g * group
+                pair = 2 * a
                 e, b = (
-                    pltpu.roll(source[f], (FINE + LANES) - shift * near, 1)[:, :width] for f in range(2)
+                    jnp.concatenate(
+                        [
+                            jnp.broadcast_to(spread_ref[g, f, pair + n : pair + n + 1, cols], (4, width))
+                            for n in range(2)
+                        ],
+                        0,
+                    )
+                    for f in range(2)
                 )
                 total.append(e * both[8 * a : 8 * a + 8] + b * both[half + 8 * a : half + 8 * a + 8])
             return jnp.concatenate(total, 0)
 
-        def put(total, cols):
-            held[g, :, :, :, cols] = total.astype(BF16).reshape(group, 2, 2, -1)
-
-        for start in range(0, row_width, FINE):
-            cols = slice(start, min(start + FINE, row_width))
-            side = (start >= M - first_pair).astype(jnp.int32)
-            put(filtered(table_rows(cols), side, start, cols.stop - start), cols)
-        start = pl.multiple_of((M - 1 - first_pair) // FINE * FINE, FINE)
-        cols = pl.ds(start, FINE)
+        def put(total, slot, cols):
+            held[slot, :, :, :, cols] = total.astype(BF16).reshape(group, 2, 2, -1)
+
+        mixed = pl.multiple_of((M - 1 - first_pair) // FINE * FINE, FINE)
+        cols = pl.ds(mixed, FINE)
         rows = table_rows(cols)
         pair = first_pair + lax.broadcasted_iota(jnp.int32, (half, FINE), 0) // 4
-        at = start + lax.broadcasted_iota(jnp.int32, (half, FINE), 1)
-        near, far = (filtered(rows, side, start, FINE) for side in range(2))
-        put(jnp.where(at < M - pair, near, far), cols)
-        copy = pltpu.make_async_copy(
-            held.at[g], out_ref.at[pl.ds(g * group, group)], sems.at[g, 2]
-        )
-        copy.start()
-        copies.append(copy)
+        at = mixed + lax.broadcasted_iota(jnp.int32, (half, FINE), 1)
+        near, far = (filtered(rows, side, cols) for side in range(2))
+        put(jnp.where(at < M - pair, near, far), g, cols)
+        sent = 0
+        for start in range(0, row_width, FINE):
+            stop = min(start + FINE, row_width)
+            cols = slice(start, stop)
+            side = (start >= M - first_pair).astype(jnp.int32)
+            slot = jnp.where(start == mixed, groups, g)
+            put(filtered(table_rows(cols), side, cols), slot, cols)
+            if stop == row_width or (stop % PIECE == 0 and row_width - stop > FINE):
+                piece = pl.ds(sent, stop - sent)
+                copy = pltpu.make_async_copy(
+                    held.at[g, :, :, :, piece],
+                    out_ref.at[pl.ds(g * group, group), :, :, piece],
+                    sems.at[g, 2 + sent // PIECE],
+                )
+                copy.start()
+                copies.append(copy)
+                sent = stop
     for copy in copies:
         copy.wait()
 
@@ -366,12 +395,12 @@
         scratch_shapes=[
             pltpu.VMEM((2, 2, cycles, 8, LANES), F32),
             pltpu.VMEM((groups, 2, 8 * group, 2 * pad_depth), BF16),
-            pltpu.VMEM((groups, group, 2, 2, row_width), BF16),
+            pltpu.VMEM((groups + 1, group, 2, 2, row_width), BF16),
             pltpu.VMEM(table_w.shape, BF16),
             pltpu.VMEM(table_x.shape, BF16),
-            pltpu.SemaphoreType.DMA((groups, 3)),
+            pltpu.SemaphoreType.DMA((groups, 2 + -(-row_width // PIECE))),
         ],
-        compiler_params=pltpu.CompilerParams(vmem_limit_bytes=56 << 20),
+        compiler_params=pltpu.CompilerParams(vmem_limit_bytes=50 << 20),
     )(modes, spread, table_w, table_x)
 
 
@@ -410,7 +439,7 @@
     modes = lax.all_to_all(payload, owners, 0, 0, tiled=True)
     if not direct:
         modes = sum_sources(modes, bands, lons)
-    spread = spread_filters(filters, per_pair)
+    spread = spread_filters(filters, per_pair, table_w.shape[1])
     return contract(modes, spread, table_w, table_x, direct)
 
 

time: 28.8 us -> 25.5 us (0.89)
  Pallas kernels: 12.7 us -> 11.1 us
  local copies, waits for them, and re-layouts: 2.13 us -> 0.73 us
    pallas_call x1, Pallas kernels: 8.21 us -> 5.51 us  [contract(): pl.pallas_call(functools.partial(contract_kernel, direct=direct), in_spec...]
    unnamed x6 -> x2, local copies, waits for them, and re-layouts: 2.13 us -> 0.73 us
    pallas_call x1, Pallas kernels: 0.31 us -> 1.34 us  [spread_filters(): pl.pallas_call(spread_kernel, in_specs=[VMEM], out_specs=VMEM, out_shape=...]
  transfers between devices with their start and end apart: 1 -> 1, of which waited for: 1 -> 1; matrix products, arithmetic and copies ran while one was open for 0% -> 0% of each run, Pallas kernels for 1% -> 5%
where the time goes in v2:
time: 25.5 us; the launch traced here: 25.2 us
  Pallas kernels  11.1 us (44%)
  starting transfers between devices  7.37 us (29%)
  waiting for transfers between devices  5.32 us (21%)
  local copies, waits for them, and re-layouts  0.73 us (3%)
  between operations  0.68 us (3%)
    all_to_all x1, starting transfers between devices, body(): modes = lax.all_to_all(payload, owners, 0, 0, tiled=True)  7.37 us
    pallas_call x1, Pallas kernels, contract(): pl.pallas_call(functools.partial(contract_kernel, direct=direct), in_spec...  5.51 us
    all_to_all x1, waiting for transfers between devices, body(): modes = lax.all_to_all(payload, owners, 0, 0, tiled=True)  5.32 us
    pallas_call x1, Pallas kernels, analyse(): pl.pallas_call(functools.partial(analyse_kernel, pad_rows=pad_rows), grid...  4.22 us
    pallas_call x1, Pallas kernels, spread_filters(): pl.pallas_call(spread_kernel, in_specs=[VMEM], out_specs=VMEM, out_shape=...  1.34 us
    unnamed x2, local copies, waits for them, and re-layouts  0.73 us
  transfers between devices with their start and end apart: 1, of which 1 were waited for; matrix products, arithmetic and copies ran while one was open for 0% of the time, Pallas kernels for 5%

profile of v2, /device:TPU:0, one launch (start us, length us, event | category | flops | bytes accessed | tf_op | source)
XLA Modules:
  0.0 25.2 jit_solution(4290601805576452062)
XLA Ops:
  0.7 4.2 %shard_map.109 = bf16[16,4,768]{2,1,0:T(4,128)(2,1)} custom-call(s32[1]{0:T(128)S(6)} %copy.12.live_ref, f32[1,2,32,128]{3,2,1,0:T(8,128)} %value_ref.1, f32[4,32,128]{2,1,0:T(8,128)} %weight_ref.1, s32[32,128]{1,0:T(8,128)} %cycle_ref.1, s32[32,128]{1,0:T(8,128)} %pixel_ref.1, bf16[256,192]{1,0:T(8,128)(2,1)} %constant.6.clone.coarse_hbm, ...), custom_call_target="tpu_custom_call" | custom-call | tf_op jit(solution)/shard_map/pallas_call | solution.py:166
  4.9 7.4 %all-to-all-start = ((bf16[16,4,768]{2,1,0:T(4,128)(2,1)}), bf16[16,4,768]{2,1,0:T(4,128)(2,1)S(1)}, u32[]{:S(2)}, u32[]{:S(2)}) async-start(bf16[16,4,768]{2,1,0:T(4,128)(2,1)} %shard_map.109), calls=%async_computation | async-start | bytes 196608 | tf_op jit(solution)/shard_map/all_to_all | solution.py:439
  12.3 0.0 copy-start
  12.3 0.7 %copy-done = f32[2,3072]{1,0:T(2,128)S(1)} copy-done((f32[2,3072]{1,0:T(2,128)S(1)}, f32[2,3072]{1,0:T(2,128)}, u32[]{:S(2)}) %copy-start) | copy-done | bytes 24600
  13.0 1.3 %shard_map.110.spread_ref = f32[3,2,32,3200]{3,2,1,0:T(8,128)S(1)} custom-call(f32[2,3072]{1,0:T(2,128)S(1)} %copy-done), custom_call_target="tpu_custom_call" | custom-call | flops 6144000 | bytes 2457600 | tf_op jit(solution)/shard_map/pallas_call | solution.py:228
  14.3 5.3 %all-to-all-done.modes_ref = bf16[16,4,768]{2,1,0:T(4,128)(2,1)S(1)} async-done(((bf16[16,4,768]{2,1,0:T(4,128)(2,1)}), bf16[16,4,768]{2,1,0:T(4,128)(2,1)S(1)}, u32[]{:S(2)}, u32[]{:S(2)}) %all-to-all-start) | async-done | bytes 98336 | tf_op jit(solution)/shard_map/all_to_all | solution.py:439
  19.7 5.5 %shard_map.111 = bf16[96,2,2,3073]{3,2,1,0:T(2,128)(2,1)} custom-call(bf16[16,4,768]{2,1,0:T(4,128)(2,1)S(1)} %all-to-all-done.modes_ref, f32[3,2,32,3200]{3,2,1,0:T(8,128)S(1)} %shard_map.110.spread_ref, bf16[96,4,3073]{2,1,0:T(4,128)(2,1)} %w_hbm.1, bf16[96,4,3073]{2,1,0:T(4,128)(2,1)} %x_hbm.1), custom_call_target="tpu_custom_call" | custom-call | tf_op jit(solution)/shard_map/pallas_call | solution.py:390
Async XLA Ops:
  4.9 14.8 %all-to-all-start = ((bf16[16,4,768]{2,1,0:T(4,128)(2,1)}), bf16[16,4,768]{2,1,0:T(4,128)(2,1)S(1)}, u32[]{:S(2)}, u32[]{:S(2)}) async-start(bf16[16,4,768]{2,1,0:T(4,128)(2,1)} %shard_map.109), calls=%async_computation | async-start | bytes 196608 | tf_op jit(solution)/shard_map/all_to_all | solution.py:439
  12.3 0.7 %copy-start = (f32[2,3072]{1,0:T(2,128)S(1)}, f32[2,3072]{1,0:T(2,128)}, u32[]{:S(2)}) copy-start(f32[2,3072]{1,0:T(2,128)} %filters_ref.1) | copy-start | bytes 73732

commit v3 on v2

--- a/solution.py
+++ b/solution.py
@@ -86,8 +86,7 @@
     cycle = cycle_ref[...]
     for dp in range(2):
         pixel = pixel_ref[...] + dp
-        index[0, dp] = (pixel >> 8).astype(F32)
-        index[1, dp] = (pixel & (FINE - 1)).astype(F32)
+        index[dp] = (pixel >> 8).astype(F32)
         for s in range(num_sims):
             value = jnp.where(alive, value_ref[0, s], 0.0)
             here = value * weight_ref[dp]
@@ -97,24 +96,29 @@
                     cycle == c, here, jnp.where(cycle == c - 1, above, 0.0)
                 )
     row_at = lax.broadcasted_iota(jnp.int32, (pad_rows, LANES), 0).astype(F32).astype(BF16)
-    fine_at = lax.broadcasted_iota(jnp.int32, (FINE, LANES), 0).astype(F32).astype(BF16)
+    fine_at = [
+        ((lax.broadcasted_iota(jnp.int32, (LANES, FINE), 1) - dp) & (FINE - 1)).astype(F32).astype(BF16)
+        for dp in range(2)
+    ]
+    fine = (pixel_ref[...] & (FINE - 1)).astype(F32).T
     one, zero = jnp.ones((), BF16), jnp.zeros((), BF16)
 
-    def all_rows(ref, n, dp, k, count):
-        row = jnp.broadcast_to(ref[n, dp, k : k + 1, :], (16, LANES)).astype(BF16)
-        return jnp.concatenate([row] * (count // 16), 0)
+    def all_rows(row):
+        row = jnp.broadcast_to(row, (16, LANES)).astype(BF16)
+        return jnp.concatenate([row] * (pad_rows // 16), 0)
 
     for k in range(rows):
+        column = jnp.broadcast_to(fine[:, k : k + 1], (LANES, LANES)).astype(BF16)
+        column = jnp.concatenate([column] * (FINE // LANES), 1)
         for dp in range(2):
             here = slice(FINE * k + LANES * dp, FINE * k + LANES * (dp + 1))
-            hit = row_at == all_rows(index, 0, dp, k, pad_rows)
+            hit = row_at == all_rows(index[dp, k : k + 1, :])
             for n in range(maps):
                 left[n * pad_rows : (n + 1) * pad_rows, here] = jnp.where(
-                    hit, all_rows(amount, n, dp, k, pad_rows), zero
+                    hit, all_rows(amount[n, dp, k : k + 1, :]), zero
                 )
-            right[:, here] = jnp.where(fine_at == all_rows(index, 1, dp, k, FINE), one, zero)
-    dims = (((1,), (1,)), ((), ()))
-    canvas = lax.dot_general(left[...], right[...], dims, preferred_element_type=F32)
+            right[here, :] = jnp.where(fine_at[dp] == column, one, zero)
+    canvas = jnp.dot(left[...], right[...], preferred_element_type=F32)
     canvas = jnp.concatenate(
         [
             jnp.concatenate(
@@ -146,6 +150,7 @@
             lanes += [real * turn_re - imag * turn_im, real * turn_im + imag * turn_re]
         blocks.append(jnp.concatenate(lanes, 1))
     turned = jnp.concatenate(blocks, 0).astype(BF16)
+    dims = (((1,), (1,)), ((), ()))
     modes = lax.dot_general(fine_ref[...], turned, dims, preferred_element_type=F32)
     half = modes.shape[0] // 2
     modes = jnp.concatenate([modes[:half], modes[half:]], 1).astype(BF16)
@@ -179,9 +184,9 @@
         out_specs=whole(out_shape),
         scratch_shapes=[
             pltpu.VMEM((maps, 2, rows, LANES), F32),
-            pltpu.VMEM((2, 2, rows, LANES), F32),
+            pltpu.VMEM((2, rows, LANES), F32),
             pltpu.VMEM((maps * pad_rows, rows * FINE), BF16),
-            pltpu.VMEM((FINE, rows * FINE), BF16),
+            pltpu.VMEM((rows * FINE, FINE), BF16),
             pltpu.VMEM(coarse.shape, BF16),
             pltpu.VMEM(twiddle.shape[1:], F32),
             pltpu.VMEM(fine.shape, BF16),
@@ -256,17 +261,18 @@
     per_pair, cycles, row_width = w_ref.shape
     group, pad_depth = grouping(per_pair, cycles)
     groups, depth, half = per_pair // group, group * cycles, 4 * group
-    tables = []
+    edges = [*range(0, row_width - FINE, PIECE), row_width]
+    tables = {}
     for g in range(groups):
-        part = pl.ds(g * group, group)
-        tables.append(
-            [
-                pltpu.make_async_copy(w_hbm.at[part], w_ref.at[part], sems.at[g, 0]),
-                pltpu.make_async_copy(x_hbm.at[part], x_ref.at[part], sems.at[g, 1]),
+        cuts = edges if g == 0 else [0, row_width]
+        for n, (first, last) in enumerate(zip(cuts, cuts[1:])):
+            part = (pl.ds(g * group, group), slice(None), pl.ds(first, last - first))
+            tables[g, first] = [
+                pltpu.make_async_copy(w_hbm.at[part], w_ref.at[part], sems.at[g, 2 * n]),
+                pltpu.make_async_copy(x_hbm.at[part], x_ref.at[part], sems.at[g, 2 * n + 1]),
             ]
-        )
-        for copy in tables[-1]:
-            copy.start()
+            for copy in tables[g, first]:
+                copy.start()
     for comp in range(2):
         for side in range(2):
             for r in range(cycles):
@@ -322,9 +328,6 @@
 
     for g in range(groups):
         first_pair = first_pair_here(per_pair) + g * group
-        for copy in tables[g]:
-            copy.wait()
-
         def table_rows(cols):
             rows = []
             for ref in (w_ref, x_ref):
@@ -355,30 +358,45 @@
         def put(total, slot, cols):
             held[slot, :, :, :, cols] = total.astype(BF16).reshape(group, 2, 2, -1)
 
+        def send(first, last):
+            piece = pl.ds(first, last - first)
+            copy = pltpu.make_async_copy(
+                held.at[g, :, :, :, piece],
+                out_ref.at[pl.ds(g * group, group), :, :, piece],
+                sems.at[g, 2 * len(edges) + first // PIECE],
+            )
+            copy.start()
+            copies.append(copy)
+
         mixed = pl.multiple_of((M - 1 - first_pair) // FINE * FINE, FINE)
-        cols = pl.ds(mixed, FINE)
-        rows = table_rows(cols)
-        pair = first_pair + lax.broadcasted_iota(jnp.int32, (half, FINE), 0) // 4
-        at = mixed + lax.broadcasted_iota(jnp.int32, (half, FINE), 1)
-        near, far = (filtered(rows, side, cols) for side in range(2))
-        put(jnp.where(at < M - pair, near, far), g, cols)
-        sent = 0
+
+        def put_mixed():
+            cols = pl.ds(mixed, FINE)
+            rows = table_rows(cols)
+            pair = first_pair + lax.broadcasted_iota(jnp.int32, (half, FINE), 0) // 4
+            at = mixed + lax.broadcasted_iota(jnp.int32, (half, FINE), 1)
+            near, far = (filtered(rows, side, cols) for side in range(2))
+            put(jnp.where(at < M - pair, near, far), g, cols)
+
+        if g > 0:
+            for copy in tables[g, 0]:
+                copy.wait()
+            put_mixed()
         for start in range(0, row_width, FINE):
+            if g == 0 and (g, start) in tables:
+                for copy in tables[g, start]:
+                    copy.wait()
             stop = min(start + FINE, row_width)
             cols = slice(start, stop)
             side = (start >= M - first_pair).astype(jnp.int32)
-            slot = jnp.where(start == mixed, groups, g)
+            slot = g if g == 0 else jnp.where(start == mixed, groups, g)
             put(filtered(table_rows(cols), side, cols), slot, cols)
-            if stop == row_width or (stop % PIECE == 0 and row_width - stop > FINE):
-                piece = pl.ds(sent, stop - sent)
-                copy = pltpu.make_async_copy(
-                    held.at[g, :, :, :, piece],
-                    out_ref.at[pl.ds(g * group, group), :, :, piece],
-                    sems.at[g, 2 + sent // PIECE],
-                )
-                copy.start()
-                copies.append(copy)
-                sent = stop
+            if g > 0 and stop in edges:
+                send(edges[edges.index(stop) - 1], stop)
+        if g == 0:
+            put_mixed()
+            for first, last in zip(edges, edges[1:]):
+                send(first, last)
     for copy in copies:
         copy.wait()
 
@@ -398,7 +416,7 @@
             pltpu.VMEM((groups + 1, group, 2, 2, row_width), BF16),
             pltpu.VMEM(table_w.shape, BF16),
             pltpu.VMEM(table_x.shape, BF16),
-            pltpu.SemaphoreType.DMA((groups, 2 + -(-row_width // PIECE))),
+            pltpu.SemaphoreType.DMA((groups, 2 * 4 + 4)),
         ],
         compiler_params=pltpu.CompilerParams(vmem_limit_bytes=50 << 20),
     )(modes, spread, table_w, table_x)

time: 25.5 us -> 24.9 us (0.976)
  Pallas kernels: 11.1 us -> 10.5 us
    pallas_call x1, Pallas kernels: 4.22 us -> 3.63 us  [analyse(): pl.pallas_call(functools.partial(analyse_kernel, pad_rows=pad_rows), grid...]
where the time goes in v3:
time: 24.9 us; the launch traced here: 24.6 us
  Pallas kernels  10.5 us (42%)
  starting transfers between devices  7.37 us (30%)
  waiting for transfers between devices  5.32 us (21%)
  local copies, waits for them, and re-layouts  0.73 us (3%)
  between operations  0.68 us (3%)
    all_to_all x1, starting transfers between devices, body(): modes = lax.all_to_all(payload, owners, 0, 0, tiled=True)  7.37 us
    pallas_call x1, Pallas kernels, contract(): pl.pallas_call(functools.partial(contract_kernel, direct=direct), in_spec...  5.49 us
    all_to_all x1, waiting for transfers between devices, body(): modes = lax.all_to_all(payload, owners, 0, 0, tiled=True)  5.32 us
    pallas_call x1, Pallas kernels, analyse(): pl.pallas_call(functools.partial(analyse_kernel, pad_rows=pad_rows), grid...  3.63 us
    pallas_call x1, Pallas kernels, spread_filters(): pl.pallas_call(spread_kernel, in_specs=[VMEM], out_specs=VMEM, out_shape=...  1.34 us
    unnamed x2, local copies, waits for them, and re-layouts  0.73 us
  transfers between devices with their start and end apart: 1, of which 1 were waited for; matrix products, arithmetic and copies ran while one was open for 0% of the time, Pallas kernels for 5%

profile of v3, /device:TPU:0, one launch (start us, length us, event | category | flops | bytes accessed | tf_op | source)
XLA Modules:
  0.0 24.6 jit_solution(3501285008992644641)
XLA Ops:
  0.7 3.6 %shard_map.109 = bf16[16,4,768]{2,1,0:T(4,128)(2,1)} custom-call(s32[1]{0:T(128)S(6)} %copy.12.live_ref, f32[1,2,32,128]{3,2,1,0:T(8,128)} %value_ref.1, f32[4,32,128]{2,1,0:T(8,128)} %weight_ref.1, s32[32,128]{1,0:T(8,128)} %cycle_ref.1, s32[32,128]{1,0:T(8,128)} %pixel_ref.1, bf16[256,192]{1,0:T(8,128)(2,1)} %constant.6.clone.coarse_hbm, ...), custom_call_target="tpu_custom_call" | custom-call | tf_op jit(solution)/shard_map/pallas_call | solution.py:171
  4.3 7.4 %all-to-all-start = ((bf16[16,4,768]{2,1,0:T(4,128)(2,1)}), bf16[16,4,768]{2,1,0:T(4,128)(2,1)S(1)}, u32[]{:S(2)}, u32[]{:S(2)}) async-start(bf16[16,4,768]{2,1,0:T(4,128)(2,1)} %shard_map.109), calls=%async_computation | async-start | bytes 196608 | tf_op jit(solution)/shard_map/all_to_all | solution.py:457
  11.7 0.0 copy-start
  11.7 0.7 %copy-done = f32[2,3072]{1,0:T(2,128)S(1)} copy-done((f32[2,3072]{1,0:T(2,128)S(1)}, f32[2,3072]{1,0:T(2,128)}, u32[]{:S(2)}) %copy-start) | copy-done | bytes 24600
  12.4 1.3 %shard_map.110.spread_ref = f32[3,2,32,3200]{3,2,1,0:T(8,128)S(1)} custom-call(f32[2,3072]{1,0:T(2,128)S(1)} %copy-done), custom_call_target="tpu_custom_call" | custom-call | flops 6144000 | bytes 2457600 | tf_op jit(solution)/shard_map/pallas_call | solution.py:233
  13.8 5.3 %all-to-all-done.modes_ref = bf16[16,4,768]{2,1,0:T(4,128)(2,1)S(1)} async-done(((bf16[16,4,768]{2,1,0:T(4,128)(2,1)}), bf16[16,4,768]{2,1,0:T(4,128)(2,1)S(1)}, u32[]{:S(2)}, u32[]{:S(2)}) %all-to-all-start) | async-done | bytes 98336 | tf_op jit(solution)/shard_map/all_to_all | solution.py:457
  19.1 5.5 %shard_map.111 = bf16[96,2,2,3073]{3,2,1,0:T(2,128)(2,1)} custom-call(bf16[16,4,768]{2,1,0:T(4,128)(2,1)S(1)} %all-to-all-done.modes_ref, f32[3,2,32,3200]{3,2,1,0:T(8,128)S(1)} %shard_map.110.spread_ref, bf16[96,4,3073]{2,1,0:T(4,128)(2,1)} %w_hbm.1, bf16[96,4,3073]{2,1,0:T(4,128)(2,1)} %x_hbm.1), custom_call_target="tpu_custom_call" | custom-call | tf_op jit(solution)/shard_map/pallas_call | solution.py:408
Async XLA Ops:
  4.3 14.8 %all-to-all-start = ((bf16[16,4,768]{2,1,0:T(4,128)(2,1)}), bf16[16,4,768]{2,1,0:T(4,128)(2,1)S(1)}, u32[]{:S(2)}, u32[]{:S(2)}) async-start(bf16[16,4,768]{2,1,0:T(4,128)(2,1)} %shard_map.109), calls=%async_computation | async-start | bytes 196608 | tf_op jit(solution)/shard_map/all_to_all | solution.py:457
  11.7 0.7 %copy-start = (f32[2,3072]{1,0:T(2,128)S(1)}, f32[2,3072]{1,0:T(2,128)}, u32[]{:S(2)}) copy-start(f32[2,3072]{1,0:T(2,128)} %filters_ref.1) | copy-start | bytes 73732
